TPU v7x, 512 devices: a whole 4x4x16 slice. The times are simulated.
512 devices in a mesh: img: 8 (over x, core), cls: 8 (over z_lo), tpl: 8 (over z_hi, y).
Axes of the slice: x: 4, y: 4, z: 16 (z_hi: 2, z_lo: 8; z = z_hi * 8 + z_lo), core: 2. Of those that a mesh axis runs over, the one named last changes fastest.
Arguments:
- images: bfloat16 [16384, 1280], P(('img', 'tpl')), may hold values from -5 to 5
- labels: int32 [16384], P(('img', 'tpl')), may hold values from 0 to 4095
- templates: bfloat16 [32, 4096, 1280], P('tpl', ('cls', 'img')), may hold values from -0.125 to 0.125
- projection: bfloat16 [1280, 1280], P('img', 'cls'), may hold values from -0.08441157 to 0.08441157
Outputs:
- grad_templates: bfloat16 [32, 4096, 1280], P('tpl', ('cls', 'img'))
- grad_projection: float32 [1280, 1280], P('img', 'cls')
All inputs are finite; a program needn't handle non-finite values.
Results may differ from a plain program's by a relative error of at most 0.011.
Values may be sent and summed in bfloat16 or wider, within the bound.
A program may use at most 64 MiB of HBM per device.

v0:
```python
import jax
import jax.numpy as jnp
from jax import lax
from jax.sharding import PartitionSpec as P

logit_scale = 50.0
epsilon = 1e-06


def inverse_norm(values):
    return lax.rsqrt(jnp.sum(values * values, axis=-1, keepdims=True) + epsilon)


def body(images, labels, templates, projection):
    tpl_count = templates.shape[0]
    cls_count = templates.shape[1]
    feat_width = templates.shape[2]
    tpl_total = tpl_count * lax.axis_size("tpl")
    img_count = lax.axis_size("img")
    wide_proj = lax.all_gather(projection, "cls", axis=1, tiled=True)
    full_proj = lax.all_gather(wide_proj, "img", axis=0, tiled=True)
    flat_tpl = templates.reshape(tpl_count * cls_count, feat_width)
    text_z = jnp.dot(flat_tpl, full_proj, preferred_element_type=jnp.float32)
    text_rz = inverse_norm(text_z)
    text_u = text_z * text_rz
    u_three = text_u.reshape(tpl_count, cls_count, feat_width)
    local_sum = jnp.sum(u_three, axis=0)
    mean_emb = lax.psum(local_sum, "tpl") / tpl_total
    mean_rn = inverse_norm(mean_emb)
    class_w = mean_emb * mean_rn
    class_b = class_w.astype(jnp.bfloat16)
    img_f = images.astype(jnp.float32)
    img_b = (img_f * inverse_norm(img_f)).astype(jnp.bfloat16)
    all_img, all_labels = (
        lax.all_gather(img_b, "img", axis=0, tiled=True),
        lax.all_gather(labels, "img", axis=0, tiled=True),
    )
    scores = logit_scale * jnp.einsum(
        "cd,nd->cn", class_b, all_img, preferred_element_type=jnp.float32
    )
    exp_scores = jnp.exp(scores)
    totals = lax.psum(jnp.sum(exp_scores, axis=0), ("img", "cls"))
    first_id = (lax.axis_index("cls") * img_count + lax.axis_index("img")) * cls_count
    class_ids = first_id + lax.broadcasted_iota(jnp.int32, (cls_count, 1), 0)
    one_hot = (all_labels[None, :] == class_ids).astype(jnp.float32)
    grad_logit = (exp_scores / totals[None, :] - one_hot).astype(jnp.bfloat16)
    partial_value = logit_scale * jnp.dot(grad_logit, all_img, preferred_element_type=jnp.float32)
    class_g = lax.psum(partial_value, "tpl")
    dot_wg = jnp.sum(class_w * class_g, axis=1, keepdims=True)
    grad_mean = (class_g - class_w * dot_wg) * mean_rn
    per_u = grad_mean / tpl_total
    inner_prod = jnp.sum(u_three * per_u[None], axis=2, keepdims=True)
    grad_z = (
        (per_u[None] - u_three * inner_prod) * text_rz.reshape(tpl_count, cls_count, 1)
    ).astype(jnp.bfloat16)
    grad_flat = grad_z.reshape(tpl_count * cls_count, feat_width)
    grad_tpl = lax.dot_general(
        grad_flat, full_proj, (((1,), (1,)), ((), ())), preferred_element_type=jnp.float32
    )
    grad_templates = grad_tpl.astype(jnp.bfloat16).reshape(tpl_count, cls_count, feat_width)
    tpl_columns = lax.all_to_all(flat_tpl, "img", split_axis=1, concat_axis=0, tiled=True)
    partial_proj = lax.dot_general(
        tpl_columns,
        lax.all_gather(grad_flat, "img", axis=0, tiled=True),
        (((0,), (0,)), ((), ())),
        preferred_element_type=jnp.float32,
    )
    shared_proj = lax.psum_scatter(
        partial_proj.astype(jnp.bfloat16), "cls", scatter_dimension=1, tiled=True
    )
    grad_projection = lax.psum(shared_proj, "tpl").astype(jnp.float32)
    return (grad_templates, grad_projection)


def solution(mesh):
    in_specs = (
        P(("img", "tpl"), None),
        P(("img", "tpl")),
        P("tpl", ("cls", "img"), None),
        P("img", "cls"),
    )
    out_specs = (P("tpl", ("cls", "img"), None), P("img", "cls"))
    return jax.shard_map(body, mesh=mesh, in_specs=in_specs, out_specs=out_specs, check_vma=False)
```

profile of v0, /device:TPU:6, one launch (start us, length us, event | category | flops | bytes accessed | tf_op | source)
XLA Modules:
  0.0 856.8 jit_solution(12290353934308617125)
XLA Ops:
  7.2 1.0 copy.10
  8.3 51.1 %all_gather.15 = bf16[160,1280]{0,1:T(8,128)(2,1)S(1)} all-gather(bf16[160,160]{0,1:T(8,128)(2,1)S(1)} %copy.10), channel_id=1, replica_groups=mesh['img'=8,'cls'=8,'tpl'=8] {'cls'}, dimensions={1}, use_global_device_ids=true | all-gather | bytes 460800 | tf_op jit(solution)/shard_map/all_gather | solution.py:20
  60.7 36.6 %all-gather.5.cloned.1.call-done = bf16[1280,1280]{1,0:T(8,128)(2,1)} async-done(((bf16[160,1280]{1,0:T(8,128)(2,1)}), bf16[1280,1280]{1,0:T(8,128)(2,1)}) %all-gather.5.cloned.1.call-update) | async-done | bytes 3276816 | tf_op jit(solution)/shard_map/all_gather | solution.py:21
  97.3 3.0 multiply_reduce_fusion
  101.5 1.0 fusion.3
  102.6 8.4 all-gather
  111.0 144.2 %all-reduce.3.cloned.1.call-done = f32[64,1280]{1,0:T(8,128)} async-done(((f32[64,1280]{1,0:T(8,128)}), f32[64,1280]{1,0:T(8,128)}) %all-reduce.3.cloned.1.call-update) | async-done | bytes 327696 | tf_op jit(solution)/shard_map/psum | solution.py:28
  255.2 1.1 multiply_reduce_fusion.2
  256.3 34.3 %all-gather.7.cloned.1.call-done = bf16[2048,1280]{1,0:T(8,128)(2,1)} async-done(((bf16[256,1280]{1,0:T(8,128)(2,1)}), bf16[2048,1280]{1,0:T(8,128)(2,1)}) %all-gather.7.cloned.1.call-update) | async-done | bytes 5242896 | tf_op jit(solution)/shard_map/all_gather | solution.py:35
  290.6 4.3 fusion.11
  294.9 204.1 %psum.29 = f32[2048]{0:T(1024)S(1)} all-reduce(f32[2048]{0:T(1024)S(1)} %get-tuple-element.6), channel_id=1, replica_groups=mesh['img'=8,'cls'=8,'tpl'=8] {'img','cls'}, use_global_device_ids=true, to_apply=%region_6.0 | all-reduce | flops 2048 | bytes 16384 | tf_op jit(solution)/shard_map/psum | solution.py:42
  499.1 4.3 convolution_multiply_fusion
  503.5 164.7 %all-reduce.5.cloned.1.call-done = f32[64,1280]{1,0:T(8,128)} async-done(((f32[64,1280]{1,0:T(8,128)}), f32[64,1280]{1,0:T(8,128)}) %all-reduce.5.cloned.1.call-update) | async-done | bytes 327696 | tf_op jit(solution)/shard_map/psum | solution.py:48
  668.1 1.2 multiply_reduce_fusion.1
  669.3 1.1 multiply_multiply_fusion
  670.7 1.1 fusion.6
  671.9 1.3 all_to_all.14
  674.2 20.7 %all_to_all.19 = bf16[256,8,160]{0,2,1:T(8,128)(2,1)S(1)} all-to-all(bf16[256,8,160]{0,2,1:T(8,128)(2,1)S(1)} %copy.12), channel_id=1, replica_groups=mesh['img'=8,'cls'=8,'tpl'=8] {'img'}, dimensions={1} | all-to-all | bytes 1310720 | tf_op jit(solution)/shard_map/all_to_all | solution.py:61
  695.0 15.7 %all-gather.9.cloned.1.call-done = bf16[2048,1280]{1,0:T(8,128)(2,1)} async-done(((bf16[256,1280]{1,0:T(8,128)(2,1)}), bf16[2048,1280]{1,0:T(8,128)(2,1)}) %all-gather.9.cloned.1.call-update) | async-done | bytes 5242896 | tf_op jit(solution)/shard_map/all_gather | solution.py:64
  710.7 3.5 fusion
  714.2 1.1 copy.14
  715.3 3.8 convolution_convert_fusion
  719.1 57.3 %reduce-scatter.4.cloned.1.call-done = bf16[160,160]{1,0:T(8,128)(2,1)} async-done(((bf16[1280,160]{1,0:T(8,128)(2,1)}), bf16[160,160]{1,0:T(8,128)(2,1)}) %reduce-scatter.4.cloned.1.call-update) | async-done | bytes 51216
  777.4 71.8 %psum.31 = bf16[160,160]{1,0:T(8,128)(2,1)S(1)} all-reduce(bf16[160,160]{1,0:T(8,128)(2,1)S(1)} %copy.15), channel_id=1, replica_groups=mesh['img'=8,'cls'=8,'tpl'=8] {'tpl'}, use_global_device_ids=true, to_apply=%region_11.0 | all-reduce | flops 25600 | bytes 102400 | tf_op jit(solution)/shard_map/psum | solution.py:71
  (37 shorter events, 5.6 us)
Async XLA Ops:
  7.2 53.3 %copy-start.1 = (bf16[256,1280]{1,0:T(8,128)(2,1)S(1)}, bf16[256,1280]{1,0:T(8,128)(2,1)}, u32[]{:S(2)}) copy-start(bf16[256,1280]{1,0:T(8,128)(2,1)} %param.4) | copy-start | bytes 1966084
  7.2 90.2 %all-gather.5.cloned.1.call-start = ((), (), s32[]{:S(2)}) async-start(), calls=%async_computation.2 | async-start | bytes 3686400 | tf_op jit(solution)/shard_map/all_gather | solution.py:21
  8.3 89.1 %copy-start.3 = (bf16[4,64,1280]{2,1,0:T(8,128)(2,1)S(1)}, bf16[4,64,1280]{2,1,0:T(8,128)(2,1)}, u32[]{:S(2)}) copy-start(bf16[4,64,1280]{2,1,0:T(8,128)(2,1)} %param.6) | copy-start | bytes 1966084
  60.4 194.7 %all-reduce.3.cloned.1.call-start = ((), (), s32[]{:S(2)}) async-start(), calls=%async_computation.3 | async-start | bytes 655360 | tf_op jit(solution)/shard_map/psum | solution.py:28
  101.4 1.2 copy-start.5
  101.4 189.1 %all-gather.7.cloned.1.call-start = ((), (), s32[]{:S(2)}) async-start(), calls=%async_computation.4 | async-start | bytes 5898240 | tf_op jit(solution)/shard_map/all_gather | solution.py:35
  102.5 565.6 %all-reduce.5.cloned.1.call-start = ((), (), s32[]{:S(2)}) async-start(), calls=%async_computation.5 | async-start | bytes 655360 | tf_op jit(solution)/shard_map/psum | solution.py:48
  499.1 169.1 %copy-start = (f32[64,1280]{1,0:T(8,128)S(1)}, f32[64,1280]{1,0:T(8,128)}, u32[]{:S(2)}) copy-start(f32[64,1280]{1,0:T(8,128)} %all-reduce.3.cloned.1.call-done) | copy-start | bytes 983044
  503.4 207.3 %all-gather.9.cloned.1.call-start = ((), (), s32[]{:S(2)}) async-start(), calls=%async_computation.6 | async-start | bytes 5898240 | tf_op jit(solution)/shard_map/all_gather | solution.py:64
  670.7 1.2 copy-start.4
  671.9 104.6 %reduce-scatter.4.cloned.1.call-start = ((), (), s32[]{:S(2)}) async-start(), calls=%async_computation.7 | async-start | bytes 737280
  714.2 1.1 copy-start.2
Sparse Core Ops, SparseCore 0:
  60.5 36.7 all-gather.4
  101.5 153.5 all-reduce.2
  258.1 32.4 all-gather.6
  503.5 164.5 all-reduce.4
  672.0 38.6 all-gather.8
  715.4 60.9 reduce-scatter.3
where the time goes:
time: 857 us
  waiting for transfers between devices  453 us (53%)
  blocking collectives  356 us (42%)
  matrix products  19 us (2%)
  between operations  14.3 us (2%)
    psum x1, blocking collectives, body(): totals = lax.psum(jnp.sum(exp_scores, axis=0), ('img', 'cls'))  204 us
    psum x1, waiting for transfers between devices, body(): class_g = lax.psum(partial_value, 'tpl')  165 us
    psum x1, waiting for transfers between devices, body(): mean_emb = lax.psum(local_sum, 'tpl') / tpl_total  144 us
    psum x1, blocking collectives, body(): grad_projection = lax.psum(shared_proj, 'tpl').astype(jnp.float32)  71.8 us
    unnamed x7, waiting for transfers between devices  57.4 us
    all_gather x1, blocking collectives, body(): wide_proj = lax.all_gather(projection, 'cls', axis=1, tiled=True)  51.1 us
    all_gather x1, waiting for transfers between devices, body(): full_proj = lax.all_gather(wide_proj, 'img', axis=0, tiled=True)  36.6 us
    all_gather x1, waiting for transfers between devices, body(): lax.all_gather(img_b, 'img', axis=0, tiled=True)  34.3 us
  transfers between devices with their start and end apart: 6, of which 6 were waited for; matrix products, arithmetic and copies ran while one was open for 1% of the time, Pallas kernels for 0%

commit v1 on v0

--- a/solution.py
+++ b/solution.py
@@ -5,6 +5,13 @@
 
 logit_scale = 50.0
 epsilon = 1e-06
+
+
+def gather_over(x, name, along):
+    devices = lax.axis_size(name)
+    blocks = jnp.stack([x for _ in range(devices)])
+    blocks = lax.all_to_all(blocks, name, split_axis=0, concat_axis=0)
+    return jnp.concatenate(blocks, axis=along)
 
 
 def inverse_norm(values):
@@ -17,7 +24,7 @@
     feat_width = templates.shape[2]
     tpl_total = tpl_count * lax.axis_size("tpl")
     img_count = lax.axis_size("img")
-    wide_proj = lax.all_gather(projection, "cls", axis=1, tiled=True)
+    wide_proj = gather_over(projection, "cls", 1)
     full_proj = lax.all_gather(wide_proj, "img", axis=0, tiled=True)
     flat_tpl = templates.reshape(tpl_count * cls_count, feat_width)
     text_z = jnp.dot(flat_tpl, full_proj, preferred_element_type=jnp.float32)

time: 857 us -> 848 us (0.989)
    all_gather x1 -> x0, blocking collectives: 51.1 us -> none  [body(): wide_proj = lax.all_gather(projection, 'cls', axis=1, tiled=True)]
    all_to_all x0 -> x1, blocking collectives: none -> 46.7 us  [gather_over(): blocks = lax.all_to_all(blocks, name, split_axis=0, concat_axis=0)]
where the time goes in v1:
time: 848 us
  waiting for transfers between devices  448 us (53%)
  blocking collectives  352 us (42%)
  matrix products  19 us (2%)
  between operations  14.3 us (2%)
    psum x1, blocking collectives, body(): totals = lax.psum(jnp.sum(exp_scores, axis=0), ('img', 'cls'))  204 us
    psum x1, waiting for transfers between devices, body(): class_g = lax.psum(partial_value, 'tpl')  165 us
    psum x1, waiting for transfers between devices, body(): mean_emb = lax.psum(local_sum, 'tpl') / tpl_total  144 us
    psum x1, blocking collectives, body(): grad_projection = lax.psum(shared_proj, 'tpl').astype(jnp.float32)  71.7 us
    unnamed x7, waiting for transfers between devices  57.4 us
    all_to_all x1, blocking collectives, gather_over(): blocks = lax.all_to_all(blocks, name, split_axis=0, concat_axis=0)  46.7 us
    all_gather x1, waiting for transfers between devices, body(): lax.all_gather(img_b, 'img', axis=0, tiled=True)  34.3 us
    all_gather x1, waiting for transfers between devices, body(): full_proj = lax.all_gather(wide_proj, 'img', axis=0, tiled=True)  31.5 us
  transfers between devices with their start and end apart: 6, of which 6 were waited for; matrix products, arithmetic and copies ran while one was open for 1% of the time, Pallas kernels for 0%

profile of v1, /device:TPU:6, one launch (start us, length us, event | category | flops | bytes accessed | tf_op | source)
XLA Modules:
  0.0 847.9 jit_solution(10681312841360047048)
XLA Ops:
  8.1 46.7 %all_to_all.24 = bf16[8,160,160]{2,1,0:T(8,128)(2,1)S(1)} all-to-all(bf16[8,160,160]{2,1,0:T(8,128)(2,1)S(1)} %stack.2), channel_id=1, replica_groups=mesh['img'=8,'cls'=8,'tpl'=8] {'cls'}, dimensions={0} | all-to-all | bytes 819200 | tf_op jit(solution)/shard_map/all_to_all | solution.py:13
  55.2 1.5 reshape.70
  57.0 31.5 %all-gather.5.cloned.1.call-done = bf16[1280,1280]{1,0:T(8,128)(2,1)} async-done(((bf16[160,1280]{1,0:T(8,128)(2,1)}), bf16[1280,1280]{1,0:T(8,128)(2,1)}) %all-gather.5.cloned.1.call-update) | async-done | bytes 3276816 | tf_op jit(solution)/shard_map/all_gather | solution.py:28
  88.4 3.0 multiply_reduce_fusion
  92.6 1.0 fusion.3
  93.7 8.4 all-gather
  102.1 144.3 %all-reduce.3.cloned.1.call-done = f32[64,1280]{1,0:T(8,128)} async-done(((f32[64,1280]{1,0:T(8,128)}), f32[64,1280]{1,0:T(8,128)}) %all-reduce.3.cloned.1.call-update) | async-done | bytes 327696 | tf_op jit(solution)/shard_map/psum | solution.py:35
  246.4 1.1 multiply_reduce_fusion.2
  247.5 34.3 %all-gather.7.cloned.1.call-done = bf16[2048,1280]{1,0:T(8,128)(2,1)} async-done(((bf16[256,1280]{1,0:T(8,128)(2,1)}), bf16[2048,1280]{1,0:T(8,128)(2,1)}) %all-gather.7.cloned.1.call-update) | async-done | bytes 5242896 | tf_op jit(solution)/shard_map/all_gather | solution.py:42
  281.8 4.3 fusion.11
  286.1 204.1 %psum.29 = f32[2048]{0:T(1024)S(1)} all-reduce(f32[2048]{0:T(1024)S(1)} %get-tuple-element.6), channel_id=1, replica_groups=mesh['img'=8,'cls'=8,'tpl'=8] {'img','cls'}, use_global_device_ids=true, to_apply=%region_6.0 | all-reduce | flops 2048 | bytes 16384 | tf_op jit(solution)/shard_map/psum | solution.py:49
  490.2 4.3 convolution_multiply_fusion
  494.6 164.7 %all-reduce.5.cloned.1.call-done = f32[64,1280]{1,0:T(8,128)} async-done(((f32[64,1280]{1,0:T(8,128)}), f32[64,1280]{1,0:T(8,128)}) %all-reduce.5.cloned.1.call-update) | async-done | bytes 327696 | tf_op jit(solution)/shard_map/psum | solution.py:55
  659.3 1.2 multiply_reduce_fusion.1
  660.5 1.1 multiply_multiply_fusion
  661.9 1.1 fusion.6
  663.2 1.3 all_to_all.18
  665.5 20.7 %all_to_all.25 = bf16[256,8,160]{0,2,1:T(8,128)(2,1)S(1)} all-to-all(bf16[256,8,160]{0,2,1:T(8,128)(2,1)S(1)} %copy.8), channel_id=1, replica_groups=mesh['img'=8,'cls'=8,'tpl'=8] {'img'}, dimensions={1} | all-to-all | bytes 1310720 | tf_op jit(solution)/shard_map/all_to_all | solution.py:68
  686.2 15.7 %all-gather.9.cloned.1.call-done = bf16[2048,1280]{1,0:T(8,128)(2,1)} async-done(((bf16[256,1280]{1,0:T(8,128)(2,1)}), bf16[2048,1280]{1,0:T(8,128)(2,1)}) %all-gather.9.cloned.1.call-update) | async-done | bytes 5242896 | tf_op jit(solution)/shard_map/all_gather | solution.py:71
  701.9 3.5 fusion
  705.4 1.1 copy.10
  706.5 3.8 convolution_convert_fusion
  710.4 57.3 %reduce-scatter.4.cloned.1.call-done = bf16[160,160]{1,0:T(8,128)(2,1)} async-done(((bf16[1280,160]{1,0:T(8,128)(2,1)}), bf16[160,160]{1,0:T(8,128)(2,1)}) %reduce-scatter.4.cloned.1.call-update) | async-done | bytes 51216
  768.6 71.7 %psum.31 = bf16[160,160]{1,0:T(8,128)(2,1)S(1)} all-reduce(bf16[160,160]{1,0:T(8,128)(2,1)S(1)} %copy.11), channel_id=1, replica_groups=mesh['img'=8,'cls'=8,'tpl'=8] {'tpl'}, use_global_device_ids=true, to_apply=%region_11.0 | all-reduce | flops 25600 | bytes 102400 | tf_op jit(solution)/shard_map/psum | solution.py:78
  (38 shorter events, 5.9 us)
Async XLA Ops:
  7.2 81.3 %all-gather.5.cloned.1.call-start = ((), (), s32[]{:S(2)}) async-start(), calls=%async_computation.3 | async-start | bytes 3686400 | tf_op jit(solution)/shard_map/all_gather | solution.py:28
  54.8 1.9 copy-start.1
  55.2 33.2 %copy-start.3 = (bf16[4,64,1280]{2,1,0:T(8,128)(2,1)S(1)}, bf16[4,64,1280]{2,1,0:T(8,128)(2,1)}, u32[]{:S(2)}) copy-start(bf16[4,64,1280]{2,1,0:T(8,128)(2,1)} %param.6) | copy-start | bytes 1966084
  56.7 189.7 %all-reduce.3.cloned.1.call-start = ((), (), s32[]{:S(2)}) async-start(), calls=%async_computation.4 | async-start | bytes 655360 | tf_op jit(solution)/shard_map/psum | solution.py:35
  92.5 1.2 copy-start.5
  92.5 189.3 %all-gather.7.cloned.1.call-start = ((), (), s32[]{:S(2)}) async-start(), calls=%async_computation.5 | async-start | bytes 5898240 | tf_op jit(solution)/shard_map/all_gather | solution.py:42
  93.6 565.7 %all-reduce.5.cloned.1.call-start = ((), (), s32[]{:S(2)}) async-start(), calls=%async_computation.6 | async-start | bytes 655360 | tf_op jit(solution)/shard_map/psum | solution.py:55
  490.2 169.1 %copy-start = (f32[64,1280]{1,0:T(8,128)S(1)}, f32[64,1280]{1,0:T(8,128)}, u32[]{:S(2)}) copy-start(f32[64,1280]{1,0:T(8,128)} %all-reduce.3.cloned.1.call-done) | copy-start | bytes 983044
  494.6 207.3 %all-gather.9.cloned.1.call-start = ((), (), s32[]{:S(2)}) async-start(), calls=%async_computation.7 | async-start | bytes 5898240 | tf_op jit(solution)/shard_map/all_gather | solution.py:71
  661.9 1.2 copy-start.4
  663.1 104.5 %reduce-scatter.4.cloned.1.call-start = ((), (), s32[]{:S(2)}) async-start(), calls=%async_computation.8 | async-start | bytes 737280
  705.4 1.1 copy-start.2
Sparse Core Ops, SparseCore 0:
  56.8 31.5 all-gather.4
  92.6 153.6 all-reduce.2
  249.3 32.4 all-gather.6
  494.7 164.5 all-reduce.4
  663.2 38.6 all-gather.8
  706.7 60.9 reduce-scatter.3
